TPU v7x, 32 devices: a whole 2x2x4 slice. The times are simulated.
32 devices in a mesh: frames: 4 (over y, x), modes: 8 (over z, core).
Axes of the slice: x: 2, y: 2, z: 4, core: 2. Of those that a mesh axis runs over, the one named last changes fastest.
Arguments:
- momentum: bfloat16 [16, 512, 512, 256], P('frames', 'modes'), may hold values from -6 to 6
- ky_list: int32 [192], replicated, may hold values from 0 to 511, as said below
- kx_list: int32 [8], replicated, may hold values from 0 to 511, as said below
- ky_gain: float32 [192], replicated, may hold values from 0.5 to 2
- kx_gain: float32 [8], replicated, may hold values from 0.5 to 2
- pair_first: int32 [8], replicated, may hold values from 0 to 3
- pair_second: int32 [8], replicated, may hold values from 0 to 3
Outputs:
- correlation: float32 [192, 8, 2, 256, 256], P('modes', 'frames')
Inputs may be any that keep to these rules, and one draw needn't show every extreme that they name: `ky_list`: 192 distinct wavenumbers. `kx_list`: 8 distinct wavenumbers.
All inputs are finite; a program needn't handle non-finite values.
Results may differ from a plain program's by a relative error of at most 0.014.
Values may be sent and summed in bfloat16 or wider, within the bound.
A program may use at most 320 MiB of HBM per device.

v0:
```python
import math

import jax
import jax.numpy as jnp
from jax import lax
from jax.sharding import PartitionSpec as P


def tables(ky_list, kx_list, ky_gain, kx_gain, grid_x, grid_y):
    y_index = jnp.arange(grid_y, dtype=jnp.int32)
    phase_y = (y_index[:, None] * ky_list[None, :] % grid_y).astype(jnp.float32) * (
        2.0 * math.pi / grid_y
    )
    y_scale = ky_gain[None, :] / math.sqrt(grid_y)
    y_table = jnp.stack([jnp.cos(phase_y) * y_scale, -jnp.sin(phase_y) * y_scale], axis=2)
    y_table = y_table.reshape(grid_y, 2 * ky_list.shape[0]).astype(jnp.bfloat16)
    x_index = jnp.arange(grid_x, dtype=jnp.int32)
    phase_x = (x_index[:, None] * kx_list[None, :] % grid_x).astype(jnp.float32) * (
        2.0 * math.pi / grid_x
    )
    x_scale = kx_gain[None, :] / math.sqrt(grid_x)
    x_table = jnp.concatenate(
        [jnp.cos(phase_x) * x_scale, jnp.sin(phase_x) * x_scale], axis=1
    ).astype(jnp.bfloat16)
    return (y_table, x_table)


def combine(column_sums):
    frame_count, col_count, mode_count, cell_count = column_sums.shape
    parted = column_sums.reshape(frame_count, col_count // 2, 2, 2, mode_count // 2, cell_count)
    real_part = parted[:, :, 0, 0] + parted[:, :, 1, 1]
    imag_part = parted[:, :, 1, 0] - parted[:, :, 0, 1]
    return jnp.stack([real_part, imag_part], axis=3)


def pair_counts(pair_first, pair_second, block_len):
    offsets = jnp.arange(block_len, dtype=jnp.int32)
    first_hot = (pair_first[:, None] == offsets[None, :]).astype(jnp.float32)
    second_hot = (pair_second[:, None] == offsets[None, :]).astype(jnp.float32)
    return jnp.dot(first_hot.T, second_hot, precision=lax.Precision.HIGHEST)


def block_matrices(counts, coeffs, pair_total):
    high = lax.Precision.HIGHEST
    weighted = jnp.einsum("ab,najkrz->nbjkrz", counts, coeffs, precision=high)
    turned = jnp.stack([coeffs[:, :, :, :, 1], -coeffs[:, :, :, :, 0]], axis=4)
    real_corr = jnp.einsum("nbjkrz,nbjkry->njkzy", weighted, coeffs, precision=high)
    imag_corr = jnp.einsum("nbjkrz,nbjkry->njkzy", weighted, turned, precision=high)
    return jnp.stack([real_corr, imag_corr], axis=3) / pair_total


def per_device(momentum, ky_list, kx_list, ky_gain, kx_gain, pair_first, pair_second):
    block_len, row_share, grid_y, cell_count = momentum.shape
    grid_x = row_share * lax.axis_size("modes")
    y_table, x_table = tables(ky_list, kx_list, ky_gain, kx_gain, grid_x, grid_y)
    planes = jnp.einsum(
        "txyz,yc->txcz", momentum, y_table, preferred_element_type=jnp.float32
    ).astype(jnp.bfloat16)
    column_sums = jnp.einsum(
        "txcz,xk->tckz",
        lax.all_to_all(planes, "modes", split_axis=2, concat_axis=1, tiled=True),
        x_table,
        preferred_element_type=jnp.float32,
    )
    modal = combine(column_sums)
    counts = pair_counts(pair_first, pair_second, block_len)
    pair_total = pair_first.shape[0]
    frame_count = block_len * lax.axis_size("frames")
    gathered = lax.all_to_all(
        modal.astype(jnp.bfloat16), "frames", split_axis=2, concat_axis=0, tiled=True
    ).astype(modal.dtype)
    centered = gathered - jnp.sum(gathered, axis=0) / frame_count
    grouped = centered.reshape((lax.axis_size("frames"), block_len) + centered.shape[1:])
    block_corr = block_matrices(counts, grouped, pair_total)
    rounded = lax.optimization_barrier(block_corr.astype(jnp.bfloat16)).astype(jnp.float32)
    return jnp.sum(rounded, axis=0)


def solution(mesh):
    in_specs = (P("frames", "modes", None, None), P(), P(), P(), P(), P(), P())
    out_specs = P("modes", "frames", None, None, None)
    return jax.shard_map(
        per_device, mesh=mesh, in_specs=in_specs, out_specs=out_specs, check_vma=False
    )
```

profile of v0, /device:TPU:0, one launch (start us, length us, event | category | flops | bytes accessed | tf_op | source)
XLA Modules:
  0.0 1451.9 jit_solution(5908619932813651842)
XLA Ops:
  0.0 0.7 broadcast_multiply_fusion.1
  0.7 2.6 multiply_convert_fusion.1
  3.3 0.4 copy.37
  3.9 56.8 %convert_bitcast_fusion = bf16[4,64,384,256]{3,2,1,0:T(8,128)(2,1)} fusion(bf16[4,64,512,256]{3,2,1,0:T(8,128)(2,1)} %param.7, bf16[512,384,1,1]{0,1,2,3:T(8,128)(2,1)S(1)} %reshape.193), kind=kOutput, calls=%fused_computation.3 | convolution fusion | flops 25794969600 | bytes 117833728 | tf_op jit(solution)/shard_map/txyz,yc->txcz/dot_general | solution.py:56
  60.7 33.9 %copy.38 = bf16[4,64,384,256]{3,1,0,2:T(8,128)(2,1)} copy(bf16[4,64,384,256]{3,2,1,0:T(8,128)(2,1)} %convert_bitcast_fusion) | data formatting | bytes 100663296 | tf_op jit(solution)/shard_map/convert_element_type | solution.py:58
  94.5 8.7 all-to-all-start
  103.4 1083.4 %all-to-all-done = bf16[4,64,384,256]{3,1,0,2:T(8,128)(2,1)} async-done(((bf16[4,64,384,256]{3,1,0,2:T(8,128)(2,1)}), bf16[4,64,384,256]{3,1,0,2:T(8,128)(2,1)}, u32[]{:S(2)}, u32[]{:S(2)}) %all-to-all-start) | async-done | bytes 50331680 | tf_op jit(solution)/shard_map/all_to_all | solution.py:61
  1186.8 33.4 %copy.39 = bf16[4,64,8,48,256]{4,1,2,3,0:T(8,128)(2,1)} copy(bf16[4,64,8,48,256]{4,1,0,3,2:T(8,128)(2,1)} %bitcast.4) | data formatting | bytes 100663296 | tf_op jit(solution)/shard_map/all_to_all | solution.py:61
  1220.2 18.8 %fusion.20 = f32[16,4,48,256]{3,0,2,1:T(8,128)S(1)} fusion(bf16[4,512,48,256]{3,1,2,0:T(8,128)(2,1)} %bitcast.53, bf16[512,8]{0,1:T(8,128)(2,1)S(1)} %get-tuple-element.14, bf16[512,8]{0,1:T(8,128)(2,1)S(1)} %get-tuple-element.13), kind=kOutput, calls=%fused_computation.43 | convolution fusion | flops 805339136 | bytes 53493760 | tf_op jit(solution)/shard_map/txcz,xk->tckz/dot_general | solution.py:59
  1239.0 0.3 fusion.30
  1239.4 1.1 fusion.11
  1240.5 0.9 pad_maximum_fusion
  1241.4 4.3 all-to-all-start.1
  1246.0 10.4 all-to-all-done.1
  1256.6 1.4 bitcast_reduce_fusion
  1258.1 1.1 bitcast_subtract_fusion
  1259.2 0.3 fusion.31
  1259.5 2.8 fusion.32
  1262.3 43.9 %convolution_bitcast_fusion.1 = f32[4,24,2,1,256,256]{5,4,2,1,0,3:T(8,128)} fusion(f32[4,4,24,2,2,256]{5,1,4,3,2,0:T(4,128)S(1)} %bitcast_subtract_fusion, f32[4,24,2,2,256,4]{4,5,3,2,1,0:T(4,128)S(1)} %fusion.32), kind=kOutput, calls=%fused_computation.5 | convolution fusion | flops 1207959552 | bytes 53477376 | tf_op jit(solution)/shard_map/nbjkrz,nbjkry->njkzy/dot_general | solution.py:47
  1306.2 0.4 fusion.41
  1306.6 44.3 %convolution_bitcast_fusion = f32[4,24,2,1,256,256]{5,4,2,1,0,3:T(8,128)} fusion(f32[4,24,2,2,256,4]{4,5,3,2,1,0:T(4,128)S(1)} %fusion.32, f32[4,4,24,2,2,256]{5,1,4,3,2,0:T(4,128)S(1)} %fusion.41), kind=kOutput, calls=%fused_computation.4 | convolution fusion | flops 1207959552 | bytes 53477376 | tf_op jit(solution)/shard_map/nbjkrz,nbjkry->njkzy/dot_general | solution.py:48
  1350.9 48.3 %fusion = bf16[4,24,2,2,256,256]{5,4,2,1,0,3:T(8,128)(2,1)} fusion(f32[4,24,2,1,256,256]{5,4,2,1,0,3:T(8,128)} %convolution_bitcast_fusion, f32[4,24,2,1,256,256]{5,4,2,1,0,3:T(8,128)} %convolution_bitcast_fusion.1), kind=kLoop, calls=%fused_computation.1 | loop fusion | flops 75497472 | bytes 150994944 | tf_op jit(solution)/shard_map/convert_element_type | solution.py:75
  1399.2 35.5 %convert_reduce_fusion = f32[24,2,2,256,256]{4,3,1,0,2:T(8,128)} fusion(bf16[4,24,2,2,256,256]{5,4,2,1,0,3:T(8,128)(2,1)} %fusion), kind=kLoop, calls=%fused_computation.2 | loop fusion | flops 44040192 | bytes 75497472 | tf_op jit(solution)/shard_map/reduce_sum | solution.py:76
  1434.7 17.3 %copy.47 = f32[24,2,2,256,256]{4,3,2,1,0:T(8,128)} copy(f32[24,2,2,256,256]{4,3,1,0,2:T(8,128)} %convert_reduce_fusion) | data formatting | bytes 50331648 | tf_op jit(solution)/shard_map/reduce_sum | solution.py:76
  (16 shorter events, 0.9 us)
Async XLA Ops:
  94.5 8.7 copy-start.1
  94.5 8.7 copy-start
  94.5 1092.2 %all-to-all-start = ((bf16[4,64,384,256]{3,1,0,2:T(8,128)(2,1)}), bf16[4,64,384,256]{3,1,0,2:T(8,128)(2,1)}, u32[]{:S(2)}, u32[]{:S(2)}) async-start(bf16[4,64,384,256]{3,1,0,2:T(8,128)(2,1)} %copy.38), calls=%async_computation | async-start | bytes 100663296 | tf_op jit(solution)/shard_map/all_to_all | solution.py:61
  1239.4 6.4 copy-start.2
  1239.4 6.4 copy-start.3
  1241.4 14.9 %all-to-all-start.1 = ((bf16[4,24,8,2,256]{4,1,3,0,2:T(8,128)(2,1)}), bf16[4,24,8,2,256]{4,1,3,0,2:T(8,128)(2,1)S(1)}, u32[]{:S(2)}, u32[]{:S(2)}) async-start(bf16[4,24,8,2,256]{4,1,3,0,2:T(8,128)(2,1)} %pad_maximum_fusion), calls=%async_computation.1 | async-start | bytes 1572864 | tf_op jit(solution)/shard_map/all_to_all | solution.py:69
where the time goes:
time: 1450 us
  waiting for transfers between devices  1090 us (75%)
  matrix products  167 us (12%)
  other arithmetic  92.7 us (6%)
  local copies, waits for them, and re-layouts  85.5 us (6%)
    all_to_all x1, waiting for transfers between devices, per_device(): lax.all_to_all(planes, 'modes', split_axis=2, concat_axis=1, tiled=True)  1080 us
    dot_general x1, matrix products, per_device(): jnp.einsum('txyz,yc->txcz', momentum, y_table, preferred_element_type=jnp...  56.8 us
    convert_element_type x1, other arithmetic, per_device(): block_corr.astype(jnp.bfloat16)  48.3 us
    dot_general x1, matrix products, block_matrices(): jnp.einsum('nbjkrz,nbjkry->njkzy', weighted, turned, precision=high)  44.3 us
    dot_general x1, matrix products, block_matrices(): jnp.einsum('nbjkrz,nbjkry->njkzy', weighted, coeffs, precision=high)  43.9 us
    reduce_sum x1, other arithmetic, per_device(): return jnp.sum(rounded, axis=0)  35.5 us
    convert_element_type x1, local copies, waits for them, and re-layouts, per_device(): planes = jnp.einsum('txyz,yc->txcz', momentum, y_table, preferred_element...  33.9 us
    all_to_all x1, local copies, waits for them, and re-layouts, per_device(): lax.all_to_all(planes, 'modes', split_axis=2, concat_axis=1, tiled=True)  33.4 us
  transfers between devices with their start and end apart: 2, of which 2 were waited for; matrix products, arithmetic and copies ran while one was open for 0% of the time, Pallas kernels for 0%

commit v1 on v0

v1 whole, which is shorter than its diff:
```python
import functools
import math

import jax
import jax.numpy as jnp
from jax import lax
from jax.experimental import pallas as pl
from jax.experimental.pallas import tpu as pltpu
from jax.sharding import PartitionSpec as P

MESH = pl.DeviceIdType.MESH
ROWS = 16
CHUNK = 64
SLOTS = 3


def wave_tables(ky_list, kx_list, ky_gain, kx_gain, x_index, grid_x, grid_y):
    y_index = jnp.arange(grid_y, dtype=jnp.int32)
    phase_y = (ky_list[:, None] * y_index[None, :] % grid_y).astype(jnp.float32) * (
        2.0 * math.pi / grid_y
    )
    y_scale = ky_gain[:, None] / math.sqrt(grid_y)
    y_cos = (jnp.cos(phase_y) * y_scale).astype(jnp.bfloat16)
    y_sin = (-jnp.sin(phase_y) * y_scale).astype(jnp.bfloat16)
    phase_x = (kx_list[:, None] * x_index[None, :] % grid_x).astype(jnp.float32) * (
        2.0 * math.pi / grid_x
    )
    x_scale = kx_gain[:, None] / math.sqrt(grid_x)
    x_cos = (jnp.cos(phase_x) * x_scale).astype(jnp.bfloat16)
    x_sin = (jnp.sin(phase_x) * x_scale).astype(jnp.bfloat16)
    return y_cos, y_sin, x_cos, x_sin


def pair_counts(pair_first, pair_second, block_len):
    offsets = jnp.arange(block_len, dtype=jnp.int32)
    first_hot = pair_first[:, None, None] == offsets[None, :, None]
    second_hot = pair_second[:, None, None] == offsets[None, None, :]
    return jnp.sum((first_hot & second_hot).astype(jnp.float32), axis=0)


def modal_kernel(
    groups, half, share,
    counts_ref, m_ref, w_ref, a_ref, z_ref,
    mbuf, ghi, glo, own, partner, outgoing, landed,
    m_sem, pair_send, pair_recv, send_sem, recv_sem,
):
    frames, _, grid_y, cells = m_ref.shape
    rows = a_ref.shape[0] // (2 * half)
    waves = groups * share
    fr = lax.axis_index("frames")
    mode = lax.axis_index("modes")
    core = lax.rem(mode, 2)
    line = lax.div(mode, 2)
    me = fr * half + line
    peers = groups * half
    other = (fr, line * 2 + 1 - core)
    chunks = grid_y // CHUNK

    def peer_at(step):
        at = lax.rem(me + step, peers)
        return at, lax.div(at, half), lax.rem(at, half)

    barrier = pltpu.get_barrier_semaphore()

    def greet(step, carry):
        _, f, l = peer_at(step)
        pl.semaphore_signal(barrier, inc=1, device_id=(f, l * 2 + core), device_id_type=MESH)
        return carry

    def load(index):
        slot = lax.rem(index, SLOTS)
        start = pl.multiple_of(lax.rem(index, chunks) * CHUNK, CHUNK)
        return pltpu.make_async_copy(
            m_ref.at[lax.div(index, chunks), :, pl.ds(start, CHUNK), :],
            mbuf.at[slot], m_sem.at[slot],
        )

    for index in range(SLOTS - 1):
        load(jnp.int32(index)).start()
    lax.fori_loop(1, peers, greet, 0)
    pl.semaphore_signal(barrier, inc=1, device_id=other, device_id_type=MESH)
    pl.semaphore_wait(barrier, peers)

    def x_chunk(t, c, carry):
        index = t * chunks + c
        load(index).wait()

        @pl.when(index + SLOTS - 1 < frames * chunks)
        def _():
            load(index + SLOTS - 1).start()

        slot = lax.rem(index, SLOTS)
        for g in range(CHUNK // ROWS):
            block = mbuf[slot, :, g * ROWS:(g + 1) * ROWS, :]
            part = jnp.dot(
                w_ref[...], block.reshape(-1, cells), preferred_element_type=jnp.float32
            )
            high = part.astype(jnp.bfloat16)
            low = (part - high.astype(jnp.float32)).astype(jnp.bfloat16)
            at = pl.ds(pl.multiple_of(c * CHUNK + g * ROWS, ROWS), ROWS)
            ghi[:, at, :] = high.reshape(2 * waves, ROWS, cells)
            glo[:, at, :] = low.reshape(2 * waves, ROWS, cells)
        return carry

    def y_wave(t, k, carry):
        f, kk = lax.div(k, share), lax.rem(k, share)
        pair = pl.ds(2 * k, 2)
        total = jnp.dot(
            a_ref[...], ghi[pair].reshape(2 * grid_y, cells), preferred_element_type=jnp.float32
        ) + jnp.dot(
            a_ref[...], glo[pair].reshape(2 * grid_y, cells), preferred_element_type=jnp.float32
        )
        own[t, :, f, kk] = total.reshape(2, half * rows, cells).astype(jnp.bfloat16)
        return carry

    def pair_copy(t):
        return pltpu.make_async_remote_copy(
            src_ref=own.at[t, 1 - core], dst_ref=partner.at[t],
            send_sem=pair_send.at[t], recv_sem=pair_recv.at[t],
            device_id=other, device_id_type=MESH,
        )

    def spread(t):
        pair_copy(t).wait()

        def add(k, carry):
            f, kk = lax.div(k, share), lax.rem(k, share)
            total = own[t, core, f, kk].astype(jnp.float32) + partner[t, f, kk].astype(jnp.float32)
            outgoing[t, f, :, kk] = total.astype(jnp.bfloat16).reshape(half, rows, cells)
            return carry

        lax.fori_loop(0, waves, add, 0)

        def send(step, carry):
            at, f, l = peer_at(step)
            pltpu.make_async_remote_copy(
                src_ref=outgoing.at[t, f, l], dst_ref=landed.at[fr, line, t],
                send_sem=send_sem.at[at], recv_sem=recv_sem.at[me],
                device_id=(f, l * 2 + core), device_id_type=MESH,
            ).start()
            return carry

        lax.fori_loop(1, peers, send, 0)
        landed[fr, line, t] = outgoing[t, fr, line]

    def frame(t, carry):
        lax.fori_loop(0, 1, functools.partial(x_chunk, t), 0)

        @pl.when(t > 0)
        def _():
            spread(t - 1)

        lax.fori_loop(1, chunks, functools.partial(x_chunk, t), 0)
        lax.fori_loop(0, waves, functools.partial(y_wave, t), 0)
        pair_copy(t).start()
        return carry

    lax.fori_loop(0, frames, frame, 0)
    spread(jnp.int32(frames - 1))

    def collect(step, carry):
        at, f, l = peer_at(step)
        pltpu.make_async_remote_copy(
            src_ref=outgoing.at[:, f, l], dst_ref=landed.at[f, l],
            send_sem=send_sem.at[at], recv_sem=recv_sem.at[at],
            device_id=(f, l * 2 + core), device_id_type=MESH,
        ).wait()
        return carry

    lax.fori_loop(1, peers, collect, 0)

    def finish(index, carry):
        kk = lax.div(index, rows // ROWS)
        at = pl.ds(pl.multiple_of(lax.rem(index, rows // ROWS) * ROWS, ROWS), ROWS)
        modal = [
            [
                jnp.sum(landed[f, :, t, kk, at, :].astype(jnp.float32), axis=0)
                for t in range(frames)
            ]
            for f in range(groups)
        ]
        mean = sum(value for block in modal for value in block) / (groups * frames)
        for f in range(groups):
            centered = [value - mean for value in modal[f]]
            for b in range(frames):
                weighted = sum(counts_ref[a, b] * centered[a] for a in range(frames))
                for first, value in ((0, weighted), (2, centered[b])):
                    high = value.astype(jnp.bfloat16)
                    low = (value - high.astype(jnp.float32)).astype(jnp.bfloat16)
                    z_ref[first, f * frames + b, kk, at, :] = high
                    z_ref[first + 1, f * frames + b, kk, at, :] = low
        return carry

    lax.fori_loop(0, share * (rows // ROWS), finish, 0)


def corr_kernel(z_ref, out_ref):
    share, _, depth, _ = z_ref.shape[1:]
    mid = depth // 2
    for kk in range(share):
        left = jnp.concatenate([z_ref[0, kk, 0], z_ref[0, kk, 1], z_ref[0, kk, 0]], axis=0)
        high, low = z_ref[0, kk, 2], z_ref[0, kk, 3]
        right = jnp.concatenate([high, high, low], axis=0)
        turned = [jnp.concatenate([v[mid:], -v[:mid]], axis=0) for v in (high, low)]
        turned = jnp.concatenate([turned[0], turned[0], turned[1]], axis=0)
        dims = (((0,), (0,)), ((), ()))
        out_ref[0, kk, 0] = lax.dot_general(left, right, dims, preferred_element_type=jnp.float32)
        out_ref[0, kk, 1] = lax.dot_general(left, turned, dims, preferred_element_type=jnp.float32)


def per_device(momentum, ky_list, kx_list, ky_gain, kx_gain, pair_first, pair_second):
    frames, row_share, grid_y, cells = momentum.shape
    groups, modes = lax.axis_size("frames"), lax.axis_size("modes")
    half = modes // 2
    wave_y, wave_x = ky_list.shape[0], kx_list.shape[0]
    per_y, share = wave_y // modes, wave_x // groups
    rows = -(-2 * per_y // ROWS) * ROWS
    x_index = lax.axis_index("modes") * row_share + jnp.arange(row_share, dtype=jnp.int32)
    y_cos, y_sin, x_cos, x_sin = wave_tables(
        ky_list, kx_list, ky_gain, kx_gain, x_index, row_share * modes, grid_y
    )
    upper = jnp.concatenate([y_cos, y_sin], axis=1)
    lower = jnp.concatenate([y_sin, -y_cos], axis=1)
    table = jnp.stack([upper, lower]).reshape(2, half, 2, per_y, 2 * grid_y)
    table = table.transpose(2, 1, 0, 3, 4).reshape(2, half, 2 * per_y, 2 * grid_y)
    table = jnp.pad(table, ((0, 0), (0, 0), (0, rows - 2 * per_y), (0, 0)))
    table = table.reshape(2 * half * rows, 2 * grid_y)
    x_rows = jnp.stack([x_cos, x_sin], axis=1).reshape(2 * wave_x, row_share)
    x_wide = jnp.repeat(jnp.repeat(x_rows, ROWS, axis=1), ROWS, axis=0)
    same = (
        lax.broadcasted_iota(jnp.int32, x_wide.shape, 0) % ROWS
        == lax.broadcasted_iota(jnp.int32, x_wide.shape, 1) % ROWS
    )
    spread_x = jnp.where(same, x_wide, jnp.zeros_like(x_wide))
    counts = pair_counts(pair_first, pair_second, frames) / pair_first.shape[0]

    bf16 = jnp.bfloat16
    vmem = pl.BlockSpec(memory_space=pltpu.VMEM)
    peers = groups * half
    parts = pl.pallas_call(
        functools.partial(modal_kernel, groups, half, share),
        out_shape=jax.ShapeDtypeStruct((4, groups * frames, share, rows, cells), bf16),
        in_specs=[
            pl.BlockSpec(memory_space=pltpu.SMEM),
            pl.BlockSpec(memory_space=pl.ANY),
            vmem,
            vmem,
        ],
        out_specs=vmem,
        scratch_shapes=[
            pltpu.VMEM((SLOTS, row_share, CHUNK, cells), bf16),
            pltpu.VMEM((2 * wave_x, grid_y, cells), bf16),
            pltpu.VMEM((2 * wave_x, grid_y, cells), bf16),
            pltpu.VMEM((frames, 2, groups, share, half * rows, cells), bf16),
            pltpu.VMEM((frames, groups, share, half * rows, cells), bf16),
            pltpu.VMEM((frames, groups, half, share, rows, cells), bf16),
            pltpu.VMEM((groups, half, frames, share, rows, cells), bf16),
            pltpu.SemaphoreType.DMA((SLOTS,)),
            pltpu.SemaphoreType.DMA((frames,)),
            pltpu.SemaphoreType.DMA((frames,)),
            pltpu.SemaphoreType.DMA((peers,)),
            pltpu.SemaphoreType.DMA((peers,)),
        ],
        compiler_params=pltpu.CompilerParams(
            collective_id=0, has_side_effects=True, vmem_limit_bytes=60 * 1024 * 1024
        ),
        name="modal",
    )(counts, momentum, spread_x, table)

    parts = parts[:, :, :, :2 * per_y].reshape(4, groups * frames, share, 2, per_y, cells)
    parts = parts.transpose(4, 2, 0, 3, 1, 5).reshape(
        per_y, share, 4, 2 * groups * frames, cells
    )
    return pl.pallas_call(
        corr_kernel,
        grid=(per_y,),
        out_shape=jax.ShapeDtypeStruct((per_y, share, 2, cells, cells), jnp.float32),
        in_specs=[pl.BlockSpec((1,) + parts.shape[1:], lambda j: (j, 0, 0, 0, 0))],
        out_specs=pl.BlockSpec((1, share, 2, cells, cells), lambda j: (j, 0, 0, 0, 0)),
        compiler_params=pltpu.CompilerParams(vmem_limit_bytes=32 * 1024 * 1024),
        name="correlate",
    )(parts)


def solution(mesh):
    in_specs = (P("frames", "modes", None, None), P(), P(), P(), P(), P(), P())
    out_specs = P("modes", "frames", None, None, None)
    return jax.shard_map(
        per_device, mesh=mesh, in_specs=in_specs, out_specs=out_specs, check_vma=False
    )
```

time: 1450 us -> 124 us (0.09)
  waiting for transfers between devices: 1090 us -> 0 us
  matrix products: 167 us -> 0 us
  Pallas kernels: 0 us -> 109 us
  other arithmetic: 92.7 us -> 8.86 us
  local copies, waits for them, and re-layouts: 85.5 us -> 5.04 us
    all_to_all x2 -> x0, waiting for transfers between devices: 1090 us -> none  [the longest x1 1080 us: per_device(): lax.all_to_all(planes, 'modes', split_axis=2, concat_axis=1, tiled=True)]
    dot_general x6 -> x0, matrix products: 167 us -> none  [the longest x1 56.8 us: per_device(): jnp.einsum('txyz,yc->txcz', momentum, y_table, preferred_element_type=jnp...]
    pallas_call x0 -> x2, Pallas kernels: none -> 109 us  [the longest x1 93.5 us: per_device(): pl.pallas_call(functools.partial(modal_kernel, groups, half, share), out_...]
    convert_element_type x2, other arithmetic: 48.5 us -> 2.65 us  [the longest x1 1.87 us: wave_tables(): y_cos = (jnp.cos(phase_y) * y_scale).astype(jnp.bfloat16)]
    reduce_sum x2 -> x1, other arithmetic: 36.8 us -> 0.09 us  [pair_counts(): return jnp.sum((first_hot & second_hot).astype(jnp.float32), axis=0)]
    convert_element_type x2 -> x0, local copies, waits for them, and re-layouts: 34 us -> none  [the longest x1 33.9 us: per_device(): planes = jnp.einsum('txyz,yc->txcz', momentum, y_table, preferred_element...]
    all_to_all x2 -> x0, local copies, waits for them, and re-layouts: 33.5 us -> none  [the longest x1 33.4 us: per_device(): lax.all_to_all(planes, 'modes', split_axis=2, concat_axis=1, tiled=True)]
    reduce_sum x1 -> x0, local copies, waits for them, and re-layouts: 17.3 us -> none  [per_device(): return jnp.sum(rounded, axis=0)]
  transfers between devices with their start and end apart: 2 -> 0, of which waited for: 2 -> 0; matrix products, arithmetic and copies ran while one was open for 0% -> 0% of each run, Pallas kernels for 0% -> 0%
where the time goes in v1:
time: 124 us; the launch traced here: 123 us
  Pallas kernels  109 us (88%)
  other arithmetic  8.86 us (7%)
  local copies, waits for them, and re-layouts  5.04 us (4%)
    pallas_call x1, Pallas kernels, per_device(): pl.pallas_call(functools.partial(modal_kernel, groups, half, share), out_...  93.5 us
    pallas_call x1, Pallas kernels, per_device(): pl.pallas_call(corr_kernel, grid=(per_y,), out_shape=jax.ShapeDtypeStruct...  15.8 us
    reshape x1, local copies, waits for them, and re-layouts, per_device(): parts[:, :, :, :2 * per_y]  3.66 us

profile of v1, /device:TPU:0, one launch (start us, length us, event | category | flops | bytes accessed | tf_op | source)
XLA Modules:
  0.0 123.3 jit_solution(17094677767091459765)
XLA Ops:
  0.0 0.7 broadcast_multiply_fusion.2
  0.7 0.7 broadcast_multiply_fusion.1
  1.3 0.7 iota_compare_fusion
  2.0 0.1 convert_reduce_fusion
  2.1 0.6 broadcast_multiply_fusion.counts_ref
  2.7 0.1 mul.162
  2.8 0.8 multiply_convert_fusion.3
  3.6 0.8 mul.156
  4.4 1.6 %fusion.7 = bf16[1,4,2,24,512]{4,3,0,1,2:T(8,128)(2,1)S(1)} fusion(f32[4,2,24]{2,0,1:T(4,128)S(1)} %copy.20, s32[4,2,24]{2,0,1:T(4,128)S(1)} %copy.19), kind=kLoop, calls=%fused_computation.14 | loop fusion | flops 1867776 | bytes 198144 | tf_op jit(solution)/shard_map/neg | solution.py:223
  5.9 0.2 broadcast_in_dim.6
  6.1 0.3 reshape.346
  6.5 1.9 %multiply_convert_fusion.1 = (bf16[1,4,2,24,512]{4,3,0,1,2:T(8,128)(2,1)S(1)}, bf16[1,4,2,24,512]{4,3,0,1,2:T(8,128)(2,1)S(1)}) fusion(f32[4,2,24]{2,0,1:T(4,128)S(1)} %copy.20, s32[4,2,24]{2,0,1:T(4,128)S(1)} %copy.19), kind=kLoop, calls=%fused_computation.10 | loop fusion | flops 1867776 | bytes 394752 | tf_op jit(solution)/shard_map/convert_element_type | solution.py:23
  8.3 1.0 maximum_maximum_fusion
  9.3 1.0 fusion.w_ref
  10.3 93.5 %modal.1 = bf16[4,16,2,48,256]{4,3,2,1,0:T(8,128)(2,1)} custom-call(f32[4,4]{1,0:T(4,128)} %broadcast_multiply_fusion.counts_ref, bf16[4,64,512,256]{3,2,1,0:T(8,128)(2,1)} %m_ref.1, bf16[256,1024]{1,0:T(8,128)(2,1)} %fusion.w_ref, bf16[384,1024]{1,0:T(8,128)(2,1)} %bitcast.12), custom_call_target="tpu_custom_call" | custom-call | tf_op jit(solution)/shard_map/modal/pallas_call | solution.py:240
  103.8 3.7 %copy.21 = bf16[4,16,2,2,24,256]{5,1,3,0,2,4:T(8,128)(2,1)S(1)} copy(bf16[4,16,2,2,24,256]{5,4,3,2,1,0:T(8,128)(2,1)} %bitcast.11) | data formatting | bytes 6291456 | tf_op jit(solution)/shard_map/reshape | solution.py:270
  107.5 15.8 %correlate.1 = f32[24,2,2,256,256]{4,3,2,1,0:T(8,128)} custom-call(bf16[24,2,4,32,256]{4,3,2,1,0:T(8,128)(2,1)S(1)} %bitcast.10), custom_call_target="tpu_custom_call" | custom-call | tf_op jit(solution)/shard_map/correlate/pallas_call | solution.py:274
  (9 shorter events, 0.0 us)

commit v2 on v1

--- a/solution.py
+++ b/solution.py
@@ -14,21 +14,9 @@
 SLOTS = 3
 
 
-def wave_tables(ky_list, kx_list, ky_gain, kx_gain, x_index, grid_x, grid_y):
-    y_index = jnp.arange(grid_y, dtype=jnp.int32)
-    phase_y = (ky_list[:, None] * y_index[None, :] % grid_y).astype(jnp.float32) * (
-        2.0 * math.pi / grid_y
-    )
-    y_scale = ky_gain[:, None] / math.sqrt(grid_y)
-    y_cos = (jnp.cos(phase_y) * y_scale).astype(jnp.bfloat16)
-    y_sin = (-jnp.sin(phase_y) * y_scale).astype(jnp.bfloat16)
-    phase_x = (kx_list[:, None] * x_index[None, :] % grid_x).astype(jnp.float32) * (
-        2.0 * math.pi / grid_x
-    )
-    x_scale = kx_gain[:, None] / math.sqrt(grid_x)
-    x_cos = (jnp.cos(phase_x) * x_scale).astype(jnp.bfloat16)
-    x_sin = (jnp.sin(phase_x) * x_scale).astype(jnp.bfloat16)
-    return y_cos, y_sin, x_cos, x_sin
+def turned_wave(product, size, quarters):
+    phase = (product + quarters * (size // 4)) % size
+    return jnp.cos(phase.astype(jnp.float32) * (2.0 * math.pi / size))
 
 
 def pair_counts(pair_first, pair_second, block_len):
@@ -41,8 +29,8 @@
 def modal_kernel(
     groups, half, share,
     counts_ref, m_ref, w_ref, a_ref, z_ref,
-    mbuf, ghi, glo, own, partner, outgoing, landed,
-    m_sem, pair_send, pair_recv, send_sem, recv_sem,
+    mbuf, ghi, glo, own, partner, outgoing, relayed, onward, landed,
+    m_sem, pair_send, pair_recv, relay_send, relay_recv, send_sem, recv_sem,
 ):
     frames, _, grid_y, cells = m_ref.shape
     rows = a_ref.shape[0] // (2 * half)
@@ -51,14 +39,24 @@
     mode = lax.axis_index("modes")
     core = lax.rem(mode, 2)
     line = lax.div(mode, 2)
-    me = fr * half + line
-    peers = groups * half
+    slots = landed.shape[0]
+    relay = slots != half
+    peers = groups * slots
+    swap = line + 1 - 2 * lax.rem(line, 2)
+    far = lax.rem(line + half // 2, half)
+    swap_far = lax.rem(swap + half // 2, half)
     other = (fr, line * 2 + 1 - core)
     chunks = grid_y // CHUNK
 
+    def line_to(slot):
+        if relay:
+            odd = lax.rem(slot, 2)
+            return odd * swap + (1 - odd) * lax.rem(line + slot, half)
+        return lax.rem(line + slot, half)
+
     def peer_at(step):
-        at = lax.rem(me + step, peers)
-        return at, lax.div(at, half), lax.rem(at, half)
+        slot, turn = lax.div(step, groups), lax.rem(step, groups)
+        return slot, lax.rem(fr + turn, groups), line_to(slot)
 
     barrier = pltpu.get_barrier_semaphore()
 
@@ -131,38 +129,85 @@
 
         lax.fori_loop(0, waves, add, 0)
 
-        def send(step, carry):
-            at, f, l = peer_at(step)
+        if relay:
+            relay_copy(t).start()
+            lax.fori_loop(1, 2 * groups, functools.partial(send, t), 0)
+        else:
+            lax.fori_loop(1, peers, functools.partial(send, t), 0)
+        landed[0, fr, t] = outgoing[t, fr, line]
+
+    def relay_copy(t):
+        return pltpu.make_async_remote_copy(
+            src_ref=outgoing.at[t, :, swap_far], dst_ref=relayed.at[t],
+            send_sem=relay_send.at[t], recv_sem=relay_recv.at[t],
+            device_id=(fr, swap * 2 + core), device_id_type=MESH,
+        )
+
+    def send(t, step, carry):
+        slot, f, l = peer_at(step)
+        pltpu.make_async_remote_copy(
+            src_ref=outgoing.at[t, f, l], dst_ref=landed.at[slot, fr, t],
+            send_sem=send_sem.at[step], recv_sem=recv_sem.at[step],
+            device_id=(f, l * 2 + core), device_id_type=MESH,
+        ).start()
+        return carry
+
+    def forward(t):
+        relay_copy(t).wait()
+
+        def add(k, carry):
+            f, kk = lax.div(k, share), lax.rem(k, share)
+            total = outgoing[t, f, far, kk].astype(jnp.float32) + relayed[t, f, kk].astype(jnp.float32)
+            onward[t, f, kk] = total.astype(jnp.bfloat16)
+            return carry
+
+        lax.fori_loop(0, waves, add, 0)
+
+        def push(turn, carry):
+            f = lax.rem(fr + turn, groups)
+            at = 2 * groups + turn
             pltpu.make_async_remote_copy(
-                src_ref=outgoing.at[t, f, l], dst_ref=landed.at[fr, line, t],
-                send_sem=send_sem.at[at], recv_sem=recv_sem.at[me],
-                device_id=(f, l * 2 + core), device_id_type=MESH,
+                src_ref=onward.at[t, f], dst_ref=landed.at[2, fr, t],
+                send_sem=send_sem.at[at], recv_sem=recv_sem.at[at],
+                device_id=(f, far * 2 + core), device_id_type=MESH,
             ).start()
             return carry
 
-        lax.fori_loop(1, peers, send, 0)
-        landed[fr, line, t] = outgoing[t, fr, line]
+        lax.fori_loop(0, groups, push, 0)
+
+    first, second = chunks // 8, chunks // 2
 
     def frame(t, carry):
-        lax.fori_loop(0, 1, functools.partial(x_chunk, t), 0)
+        lax.fori_loop(0, first, functools.partial(x_chunk, t), 0)
 
         @pl.when(t > 0)
         def _():
             spread(t - 1)
 
-        lax.fori_loop(1, chunks, functools.partial(x_chunk, t), 0)
+        lax.fori_loop(first, second, functools.partial(x_chunk, t), 0)
+        if relay:
+
+            @pl.when(t > 0)
+            def _():
+                forward(t - 1)
+
+        lax.fori_loop(second, chunks, functools.partial(x_chunk, t), 0)
         lax.fori_loop(0, waves, functools.partial(y_wave, t), 0)
         pair_copy(t).start()
         return carry
 
     lax.fori_loop(0, frames, frame, 0)
     spread(jnp.int32(frames - 1))
+    if relay:
+        forward(jnp.int32(frames - 1))
 
     def collect(step, carry):
-        at, f, l = peer_at(step)
+        slot, f, l = peer_at(step)
+        source = lax.rem(fr + groups - lax.rem(step, groups), groups)
+        block = landed.at[slot, source]
         pltpu.make_async_remote_copy(
-            src_ref=outgoing.at[:, f, l], dst_ref=landed.at[f, l],
-            send_sem=send_sem.at[at], recv_sem=recv_sem.at[at],
+            src_ref=block, dst_ref=block,
+            send_sem=send_sem.at[step], recv_sem=recv_sem.at[step],
             device_id=(f, l * 2 + core), device_id_type=MESH,
         ).wait()
         return carry
@@ -174,7 +219,7 @@
         at = pl.ds(pl.multiple_of(lax.rem(index, rows // ROWS) * ROWS, ROWS), ROWS)
         modal = [
             [
-                jnp.sum(landed[f, :, t, kk, at, :].astype(jnp.float32), axis=0)
+                jnp.sum(landed[:, f, t, kk, at, :].astype(jnp.float32), axis=0)
                 for t in range(frames)
             ]
             for f in range(groups)
@@ -195,17 +240,23 @@
 
 
 def corr_kernel(z_ref, out_ref):
-    share, _, depth, _ = z_ref.shape[1:]
+    many, share, _, depth, _ = z_ref.shape
     mid = depth // 2
-    for kk in range(share):
-        left = jnp.concatenate([z_ref[0, kk, 0], z_ref[0, kk, 1], z_ref[0, kk, 0]], axis=0)
-        high, low = z_ref[0, kk, 2], z_ref[0, kk, 3]
-        right = jnp.concatenate([high, high, low], axis=0)
-        turned = [jnp.concatenate([v[mid:], -v[:mid]], axis=0) for v in (high, low)]
-        turned = jnp.concatenate([turned[0], turned[0], turned[1]], axis=0)
-        dims = (((0,), (0,)), ((), ()))
-        out_ref[0, kk, 0] = lax.dot_general(left, right, dims, preferred_element_type=jnp.float32)
-        out_ref[0, kk, 1] = lax.dot_general(left, turned, dims, preferred_element_type=jnp.float32)
+    for j in range(many):
+        for kk in range(share):
+            left = jnp.concatenate([z_ref[j, kk, 0], z_ref[j, kk, 1], z_ref[j, kk, 0]], axis=0)
+            high, low = z_ref[j, kk, 2], z_ref[j, kk, 3]
+            both = [
+                jnp.concatenate([v, jnp.concatenate([v[mid:], -v[:mid]], axis=0)], axis=1)
+                for v in (high, low)
+            ]
+            result = lax.dot_general(
+                left, jnp.concatenate([both[0], both[0], both[1]], axis=0),
+                (((0,), (0,)), ((), ())), preferred_element_type=jnp.float32,
+            )
+            cells = result.shape[0]
+            out_ref[j, kk, 0] = result[:, :cells]
+            out_ref[j, kk, 1] = result[:, cells:]
 
 
 def per_device(momentum, ky_list, kx_list, ky_gain, kx_gain, pair_first, pair_second):
@@ -215,28 +266,34 @@
     wave_y, wave_x = ky_list.shape[0], kx_list.shape[0]
     per_y, share = wave_y // modes, wave_x // groups
     rows = -(-2 * per_y // ROWS) * ROWS
-    x_index = lax.axis_index("modes") * row_share + jnp.arange(row_share, dtype=jnp.int32)
-    y_cos, y_sin, x_cos, x_sin = wave_tables(
-        ky_list, kx_list, ky_gain, kx_gain, x_index, row_share * modes, grid_y
-    )
-    upper = jnp.concatenate([y_cos, y_sin], axis=1)
-    lower = jnp.concatenate([y_sin, -y_cos], axis=1)
-    table = jnp.stack([upper, lower]).reshape(2, half, 2, per_y, 2 * grid_y)
-    table = table.transpose(2, 1, 0, 3, 4).reshape(2, half, 2 * per_y, 2 * grid_y)
-    table = jnp.pad(table, ((0, 0), (0, 0), (0, rows - 2 * per_y), (0, 0)))
-    table = table.reshape(2 * half * rows, 2 * grid_y)
-    x_rows = jnp.stack([x_cos, x_sin], axis=1).reshape(2 * wave_x, row_share)
-    x_wide = jnp.repeat(jnp.repeat(x_rows, ROWS, axis=1), ROWS, axis=0)
-    same = (
-        lax.broadcasted_iota(jnp.int32, x_wide.shape, 0) % ROWS
-        == lax.broadcasted_iota(jnp.int32, x_wide.shape, 1) % ROWS
-    )
-    spread_x = jnp.where(same, x_wide, jnp.zeros_like(x_wide))
+    grid_x = row_share * modes
+
+    def by_owner(values):
+        values = values.reshape(half, 2, 1, per_y).transpose(1, 0, 2, 3)
+        values = jnp.broadcast_to(values, (2, half, 2, per_y)).reshape(2, half, 2 * per_y)
+        return jnp.pad(values, ((0, 0), (0, 0), (0, rows - 2 * per_y))).reshape(-1, 1)
+
+    shape = (2 * half * rows, 2 * grid_y)
+    row = lax.broadcasted_iota(jnp.int32, shape, 0) % rows
+    column = lax.broadcasted_iota(jnp.int32, shape, 1)
+    quarters = (row >= per_y).astype(jnp.int32) + (column >= grid_y).astype(jnp.int32)
+    table = turned_wave(by_owner(ky_list) * (column % grid_y), grid_y, quarters)
+    table = (table * (by_owner(ky_gain) / math.sqrt(grid_y))).astype(jnp.bfloat16)
+
+    shape = (2 * wave_x * ROWS, row_share * ROWS)
+    row = lax.broadcasted_iota(jnp.int32, shape, 0)
+    column = lax.broadcasted_iota(jnp.int32, shape, 1)
+    x_index = lax.axis_index("modes") * row_share + column // ROWS
+    kx_rows = jnp.repeat(kx_list, 2 * ROWS)[:, None]
+    kx_scale = jnp.repeat(kx_gain, 2 * ROWS)[:, None] / math.sqrt(grid_x)
+    spread_x = turned_wave(kx_rows * x_index, grid_x, row // ROWS % 2 * 3) * kx_scale
+    spread_x = jnp.where(row % ROWS == column % ROWS, spread_x, 0.0).astype(jnp.bfloat16)
     counts = pair_counts(pair_first, pair_second, frames) / pair_first.shape[0]
 
     bf16 = jnp.bfloat16
     vmem = pl.BlockSpec(memory_space=pltpu.VMEM)
-    peers = groups * half
+    slots = 3 if half == 4 else half
+    peers = groups * slots
     parts = pl.pallas_call(
         functools.partial(modal_kernel, groups, half, share),
         out_shape=jax.ShapeDtypeStruct((4, groups * frames, share, rows, cells), bf16),
@@ -254,8 +311,12 @@
             pltpu.VMEM((frames, 2, groups, share, half * rows, cells), bf16),
             pltpu.VMEM((frames, groups, share, half * rows, cells), bf16),
             pltpu.VMEM((frames, groups, half, share, rows, cells), bf16),
-            pltpu.VMEM((groups, half, frames, share, rows, cells), bf16),
+            pltpu.VMEM((frames, groups, share, rows, cells), bf16),
+            pltpu.VMEM((frames, groups, share, rows, cells), bf16),
+            pltpu.VMEM((slots, groups, frames, share, rows, cells), bf16),
             pltpu.SemaphoreType.DMA((SLOTS,)),
+            pltpu.SemaphoreType.DMA((frames,)),
+            pltpu.SemaphoreType.DMA((frames,)),
             pltpu.SemaphoreType.DMA((frames,)),
             pltpu.SemaphoreType.DMA((frames,)),
             pltpu.SemaphoreType.DMA((peers,)),
@@ -271,12 +332,13 @@
     parts = parts.transpose(4, 2, 0, 3, 1, 5).reshape(
         per_y, share, 4, 2 * groups * frames, cells
     )
+    many = 3 if per_y % 3 == 0 else 1
     return pl.pallas_call(
         corr_kernel,
-        grid=(per_y,),
+        grid=(per_y // many,),
         out_shape=jax.ShapeDtypeStruct((per_y, share, 2, cells, cells), jnp.float32),
-        in_specs=[pl.BlockSpec((1,) + parts.shape[1:], lambda j: (j, 0, 0, 0, 0))],
-        out_specs=pl.BlockSpec((1, share, 2, cells, cells), lambda j: (j, 0, 0, 0, 0)),
+        in_specs=[pl.BlockSpec((many,) + parts.shape[1:], lambda j: (j, 0, 0, 0, 0))],
+        out_specs=pl.BlockSpec((many, share, 2, cells, cells), lambda j: (j, 0, 0, 0, 0)),
         compiler_params=pltpu.CompilerParams(vmem_limit_bytes=32 * 1024 * 1024),
         name="correlate",
     )(parts)

time: 124 us -> 124 us (level)
  Pallas kernels: 109 us -> 102 us
  other arithmetic: 8.86 us -> 15.5 us
    convert_element_type x2, other arithmetic: 2.65 us -> 12.7 us  [the longest x1 7.41 us: per_device(): (table * (by_owner(ky_gain) / math.sqrt(grid_y))).astype(jnp.bfloat16)]
    pallas_call x1, Pallas kernels: 15.8 us -> 10.1 us  [per_device(): pl.pallas_call(corr_kernel, grid=(per_y // many,), out_shape=jax.ShapeDty...]
    neg x1 -> x0, other arithmetic: 1.55 us -> none  [per_device(): lower = jnp.concatenate([y_sin, -y_cos], axis=1)]
where the time goes in v2:
time: 124 us
  Pallas kernels  102 us (82%)
  other arithmetic  15.5 us (12%)
  local copies, waits for them, and re-layouts  5.69 us (5%)
    pallas_call x1, Pallas kernels, per_device(): pl.pallas_call(functools.partial(modal_kernel, groups, half, share), out_...  92.3 us
    pallas_call x1, Pallas kernels, per_device(): pl.pallas_call(corr_kernel, grid=(per_y // many,), out_shape=jax.ShapeDty...  10.1 us
    convert_element_type x1, other arithmetic, per_device(): (table * (by_owner(ky_gain) / math.sqrt(grid_y))).astype(jnp.bfloat16)  7.41 us
    convert_element_type x1, other arithmetic, per_device(): jnp.where(row % ROWS == column % ROWS, spread_x, 0.0).astype(jnp.bfloat16)  5.34 us
    reshape x1, local copies, waits for them, and re-layouts, per_device(): parts[:, :, :, :2 * per_y]  3.66 us

profile of v2, /device:TPU:0, one launch (start us, length us, event | category | flops | bytes accessed | tf_op | source)
XLA Modules:
  0.0 123.6 jit_solution(13439972211300744563)
XLA Ops:
  0.0 0.7 broadcast_multiply_fusion.2
  0.7 0.7 broadcast_multiply_fusion.1
  1.3 0.7 iota_compare_fusion.1
  2.0 0.1 convert_reduce_fusion
  2.1 0.6 broadcast_multiply_fusion.counts_ref
  2.8 0.1 div.51
  2.9 0.1 broadcast_in_dim.27
  2.9 0.1 div.48
  3.0 0.1 div.54
  3.1 0.8 reshape.86
  3.9 0.1 mul.75
  4.0 0.7 broadcast_in_dim.26
  4.7 0.1 mul.65
  4.8 5.3 %fusion.14.w_ref = bf16[256,1024]{1,0:T(8,128)(2,1)} fusion(f32[256]{0:T(256)S(1)} %div.48, s32[256]{0:T(256)S(1)} %get-tuple-element.15, s32[256]{0:T(256)S(1)} %get-tuple-element.18, s32[1024]{0:T(1024)S(1)} %get-tuple-element.7, s32[1024]{0:T(1024)S(1)} %get-tuple-element.10, s32[]{:T(128)S(6)} %mul.67, s32[256]{0:T(256)S(1)} %mul.65, ...), kind=kLoop, calls=%fused_computation.26 | loop fusion | flops 9437184 | bytes 549380 | tf_op jit(solution)/shard_map/convert_element_type | solution.py:290
  10.2 7.4 %fusion.5.a_ref = bf16[384,1024]{1,0:T(8,128)(2,1)} fusion(f32[384]{0:T(512)S(1)} %div.54, s32[1024]{0:T(1024)S(1)} %get-tuple-element.22, s32[384]{0:T(512)S(1)} %get-tuple-element.23, s32[384]{0:T(512)S(1)} %get-tuple-element.24, s32[1024]{0:T(1024)S(1)} %get-tuple-element.19, s32[1024]{0:T(1024)S(1)} %get-tuple-element.20, s32[384]{0:T(512)S(1)} %mul.75, ...), kind=kLoop, calls=%fused_computation.11 | loop fusion | flops 9043968 | bytes 806272 | tf_op jit(solution)/shard_map/convert_element_type | solution.py:281
  17.6 92.3 %modal.1 = bf16[4,16,2,48,256]{4,3,2,1,0:T(8,128)(2,1)} custom-call(f32[4,4]{1,0:T(4,128)} %broadcast_multiply_fusion.counts_ref, bf16[4,64,512,256]{3,2,1,0:T(8,128)(2,1)} %m_ref.1, bf16[256,1024]{1,0:T(8,128)(2,1)} %fusion.14.w_ref, bf16[384,1024]{1,0:T(8,128)(2,1)} %fusion.5.a_ref), custom_call_target="tpu_custom_call" | custom-call | tf_op jit(solution)/shard_map/modal/pallas_call | solution.py:297
  109.9 3.7 %copy.13 = bf16[4,16,2,2,24,256]{5,1,3,0,2,4:T(8,128)(2,1)S(1)} copy(bf16[4,16,2,2,24,256]{5,4,3,2,1,0:T(8,128)(2,1)} %bitcast.11) | data formatting | bytes 6291456 | tf_op jit(solution)/shard_map/reshape | solution.py:331
  113.6 10.1 %correlate.1 = f32[24,2,2,256,256]{4,3,2,1,0:T(8,128)} custom-call(bf16[24,2,4,32,256]{4,3,2,1,0:T(8,128)(2,1)S(1)} %bitcast.10), custom_call_target="tpu_custom_call" | custom-call | tf_op jit(solution)/shard_map/correlate/pallas_call | solution.py:336
  (14 shorter events, 0.1 us)
